TPU v7x, 512 devices: a whole 4x8x8 slice. The times are simulated.
512 devices in a mesh: dp: 16 (over z, core), tensor: 32 (over x, y).
Axes of the slice: x: 4, y: 8, z: 8, core: 2. Of those that a mesh axis runs over, the one named last changes fastest.
Arguments:
- activations: bfloat16 [12288, 4096], P('dp', 'tensor'), may hold values from -6 to 6
- out_grads_t: bfloat16 [5504, 12288], P('tensor', 'dp'), may hold values from -6 to 6
- in_basis: bfloat16 [4096, 4096], P(None, 'tensor'), may hold values from -0.09375 to 0.09375
- out_basis_t: bfloat16 [5504, 5504], P('tensor'), may hold values from -0.078125 to 0.078125
- query_proj: bfloat16 [4, 5504, 4096], P(None, 'tensor', 'dp'), may hold values from -6 to 6
- eigvals: float32 [5504, 4096], P('tensor', 'dp'), may hold values from 0.05 to 5
- damping: float32 [1], replicated, may hold values from 0.05 to 0.2
- lengths: int32 [96], P('dp'), may hold values from 1 to 128, 7680 in all
Outputs:
- scores: float32 [96, 4], P('dp')
Inputs may be any that keep to these rules, and one draw needn't show every extreme that they name: `lengths`: the largest token count is exactly 128.
All inputs are finite; a program needn't handle non-finite values. No bound on the sum of `lengths` on one device may be relied on, other than what follows from the above.
Results may differ from a plain program's by a relative error of at most 0.006.
Values may be sent and summed in bfloat16 or wider, within the bound.
No kernel may reach another device: no remote copies, remote signals or barrier semaphores. Data moves between devices by JAX's collectives and lax.ppermute only.
A program may use at most 128 MiB of HBM per device.

v0:
```python
import jax
import jax.numpy as jnp
from jax import lax
from jax.sharding import PartitionSpec as P


def local(activations, out_grads_t, in_basis, out_basis_t, query_proj, eigvals, damping, lengths):
    full_act = lax.all_gather(activations, "tensor", axis=1, tiled=True)
    act_local = jnp.dot(full_act, in_basis, preferred_element_type=jnp.float32).astype(jnp.bfloat16)
    act_proj = lax.all_gather(act_local, "tensor", axis=1, tiled=True)
    token_rows = full_act.shape[0]
    width = out_basis_t.shape[0]
    grad_full = jnp.dot(
        out_basis_t,
        lax.all_gather(out_grads_t, "tensor", axis=0, tiled=True),
        preferred_element_type=jnp.float32,
    )
    seq_count = lengths.shape[0]
    seq_len = token_rows // seq_count
    position = lax.broadcasted_iota(jnp.int32, (seq_count, seq_len), 1)
    keep = (position < lengths[:, None]).astype(jnp.float32).reshape(1, token_rows)
    grad_proj = (grad_full * keep).astype(jnp.bfloat16)
    scaled = (query_proj.astype(jnp.float32) / (eigvals + damping[0])).astype(jnp.bfloat16)
    projected = jnp.einsum(
        "jst,std->sjd",
        grad_proj.reshape(width, seq_count, seq_len),
        act_proj.reshape(seq_count, seq_len, act_proj.shape[1]),
        preferred_element_type=jnp.float32,
    )
    partial_value = jnp.einsum(
        "sij,qij->sq",
        projected,
        lax.all_gather(scaled, "dp", axis=2, tiled=True).astype(jnp.float32),
    )
    totals = lax.psum(partial_value, "tensor")
    norm_factor = (act_proj.shape[1] * out_basis_t.shape[1] * seq_len) ** (-0.5)
    return totals * norm_factor


def solution(mesh):
    placed = (
        P("dp", "tensor"),
        P("tensor", "dp"),
        P(None, "tensor"),
        P("tensor", None),
        P(None, "tensor", "dp"),
        P("tensor", "dp"),
        P(),
        P("dp"),
    )
    return jax.shard_map(
        local, mesh=mesh, in_specs=placed, out_specs=P("dp", None), check_vma=False
    )
```

profile of v0, /device:TPU:64, one launch (start us, length us, event | category | flops | bytes accessed | tf_op | source)
XLA Modules:
  0.0 474.7 jit_solution(10755105774203012612)
XLA Ops:
  6.5 0.0 copy-start
  6.5 0.0 copy-start.2
  6.5 0.0 copy-start.1
  6.5 0.0 copy-start.3
  6.5 0.0 all-gather.6.cloned.1.call-start
  6.6 0.7 all-gather.6.cloned.1.call-update
  7.3 0.0 all-gather.12.cloned.1.call-start
  7.3 0.7 all-gather.12.cloned.1.call-update
  8.0 0.0 all-gather.8.cloned.1.call-start
  8.1 104.2 %all-gather.6.cloned.1.call-done = bf16[768,4096]{1,0:T(8,128)(2,1)} async-done(((bf16[768,128]{1,0:T(8,128)(2,1)}), bf16[768,4096]{1,0:T(8,128)(2,1)}) %all-gather.6.cloned.1.call-update) | async-done | bytes 6291472 | tf_op jit(solution)/shard_map/all_gather | solution.py:8
  112.3 5.5 %convolution_convert_fusion = bf16[768,128]{1,0:T(8,128)(2,1)} fusion(bf16[768,4096]{1,0:T(8,128)(2,1)} %all-gather.6.cloned.1.call-done, bf16[4096,128]{1,0:T(8,128)(2,1)} %param.10), kind=kOutput, calls=%fused_computation.4 | convolution fusion | flops 805404672 | bytes 7536640 | tf_op jit(solution)/shard_map/dot_general | solution.py:9
  117.8 0.0 all-gather.8.cloned.1.call-update
  117.8 0.0 all-gather.10.cloned.1.call-start
  118.5 0.0 copy-done.2
  118.5 0.0 copy-done.1
  118.5 0.9 fusion.6
  119.5 0.0 all-gather.10.cloned.1.call-update
  119.5 0.0 copy-done.3
  119.5 0.1 convert_bitcast_fusion
  119.6 100.5 %all-gather.12.cloned.1.call-done = bf16[32,172,768]{2,1,0:T(8,128)(2,1)} async-done(((bf16[1,172,768]{2,1,0:T(8,128)(2,1)}), bf16[32,172,768]{2,1,0:T(8,128)(2,1)}) %all-gather.12.cloned.1.call-update) | async-done | bytes 8454160 | tf_op jit(solution)/shard_map/all_gather | solution.py:15
  220.1 12.5 %reshape.30 = bf16[5504,768]{1,0:T(8,128)(2,1)} reshape(bf16[32,172,768]{2,1,0:T(8,128)(2,1)} %all-gather.12.cloned.1.call-done) | data formatting | bytes 16908288
  232.6 0.0 copy-done
  232.6 5.2 %fusion.2 = bf16[172,768]{1,0:T(8,128)(2,1)S(1)} fusion(bf16[172,5504]{1,0:T(8,128)(2,1)S(1)} %copy-done, bf16[5504,768]{1,0:T(8,128)(2,1)} %reshape.30, f32[768]{0:T(1024)S(1)} %convert_bitcast_fusion), kind=kOutput, calls=%fused_computation.3 | convolution fusion | flops 1454376960 | bytes 10614784 | tf_op jit(solution)/shard_map/dot_general | solution.py:13
  237.7 0.3 reshape.26
  238.0 80.5 %all-gather.8.cloned.1.call-done = bf16[768,4096]{1,0:T(8,128)(2,1)} async-done(((bf16[768,128]{1,0:T(8,128)(2,1)}), bf16[768,4096]{1,0:T(8,128)(2,1)}) %all-gather.8.cloned.1.call-update) | async-done | bytes 6291472 | tf_op jit(solution)/shard_map/all_gather | solution.py:10
  318.6 8.5 %fusion.7 = bf16[6,172,4096]{2,1,0:T(8,128)(2,1)} fusion(bf16[6,128,4096]{2,1,0:T(8,128)(2,1)} %bitcast.14, bf16[172,6,128]{2,1,0:T(8,128)(2,1)S(1)} %reshape.26), kind=kOutput, calls=%fused_computation.8 | convolution fusion | flops 1082130432 | bytes 15009792 | tf_op jit(solution)/shard_map/jst,std->sjd/dot_general | solution.py:24
  327.1 51.2 %all-gather.10.cloned.1.call-done = bf16[4,172,4096]{2,0,1:T(4,128)(2,1)} async-done(((bf16[4,172,256]{2,0,1:T(4,128)(2,1)}), bf16[4,172,4096]{2,0,1:T(4,128)(2,1)}) %all-gather.10.cloned.1.call-update) | async-done | bytes 5636112 | tf_op jit(solution)/shard_map/all_gather | solution.py:33
  378.3 15.5 %fusion.3 = f32[6,4]{0,1:T(4,128)S(1)} fusion(bf16[4,172,4096]{2,0,1:T(4,128)(2,1)} %all-gather.10.cloned.1.call-done, bf16[6,172,4096]{2,1,0:T(8,128)(2,1)} %fusion.7), kind=kOutput, calls=%fused_computation.5 | convolution fusion | flops 33816576 | bytes 14090336 | tf_op jit(solution)/shard_map/sij,qij->sq/dot_general | solution.py:30
  393.8 73.8 %psum.7 = f32[6,4]{0,1:T(4,128)S(1)} all-reduce(f32[6,4]{0,1:T(4,128)S(1)} %fusion.3), channel_id=1, replica_groups=mesh['dp'=16,'tensor'=32] {'tensor'}, use_global_device_ids=true, to_apply=%region_0.0 | all-reduce | flops 24 | bytes 192 | tf_op jit(solution)/shard_map/psum | solution.py:35
  467.6 0.6 broadcast_multiply_fusion
  (1 shorter events, 0.0 us)
Async XLA Ops:
  6.5 226.0 %copy-start = (bf16[172,5504]{1,0:T(8,128)(2,1)S(1)}, bf16[172,5504]{1,0:T(8,128)(2,1)}, u32[]{:S(2)}) copy-start(bf16[172,5504]{1,0:T(8,128)(2,1)} %param.11) | copy-start | bytes 5680132
  6.5 111.9 %copy-start.2 = (f32[172,256]{1,0:T(8,128)S(1)}, f32[172,256]{1,0:T(8,128)}, u32[]{:S(2)}) copy-start(f32[172,256]{1,0:T(8,128)} %param.13) | copy-start | bytes 528388
  6.5 112.0 %copy-start.1 = (bf16[4,172,256]{2,0,1:T(4,128)(2,1)S(1)}, bf16[4,172,256]{2,0,1:T(4,128)(2,1)}, u32[]{:S(2)}) copy-start(bf16[4,172,256]{2,0,1:T(4,128)(2,1)} %param.12) | copy-start | bytes 1056772
  6.5 112.9 %copy-start.3 = (s32[6]{0:T(128)S(1)}, s32[6]{0:T(128)}, u32[]{:S(2)}) copy-start(s32[6]{0:T(128)} %param.15) | copy-start | bytes 76
  6.5 105.7 %all-gather.6.cloned.1.call-start = ((), (), s32[]{:S(2)}) async-start(), calls=%async_computation | async-start | bytes 6488064 | tf_op jit(solution)/shard_map/all_gather | solution.py:8
  7.3 212.8 %all-gather.12.cloned.1.call-start = ((), (), s32[]{:S(2)}) async-start(), calls=%async_computation.3 | async-start | bytes 8921088 | tf_op jit(solution)/shard_map/all_gather | solution.py:15
  8.0 310.6 %all-gather.8.cloned.1.call-start = ((), (), s32[]{:S(2)}) async-start(), calls=%async_computation.1 | async-start | bytes 6488064 | tf_op jit(solution)/shard_map/all_gather | solution.py:10
  117.8 260.5 %all-gather.10.cloned.1.call-start = ((), (), s32[]{:S(2)}) async-start(), calls=%async_computation.2 | async-start | bytes 5988352 | tf_op jit(solution)/shard_map/all_gather | solution.py:33
Sparse Core Ops, SparseCore 0:
  10.4 101.8 all-gather.5
  115.4 104.6 all-gather.11
  223.1 95.4 all-gather.7
  320.5 57.7 all-gather.9
where the time goes:
time: 475 us
  waiting for transfers between devices  338 us (71%)
  blocking collectives  73.8 us (16%)
  matrix products  34.7 us (7%)
  between operations  13.8 us (3%)
  local copies, waits for them, and re-layouts  12.8 us (3%)
    all_gather x1, waiting for transfers between devices, local(): full_act = lax.all_gather(activations, 'tensor', axis=1, tiled=True)  104 us
    all_gather x1, waiting for transfers between devices, local(): lax.all_gather(out_grads_t, 'tensor', axis=0, tiled=True)  101 us
    all_gather x1, waiting for transfers between devices, local(): act_proj = lax.all_gather(act_local, 'tensor', axis=1, tiled=True)  80.5 us
    psum x1, blocking collectives, local(): totals = lax.psum(partial_value, 'tensor')  73.8 us
    all_gather x1, waiting for transfers between devices, local(): lax.all_gather(scaled, 'dp', axis=2, tiled=True).astype(jnp.float32)  51.2 us
    dot_general x1, matrix products, local(): jnp.einsum('sij,qij->sq', projected, lax.all_gather(scaled, 'dp', axis=2,...  15.5 us
    unnamed x9, local copies, waits for them, and re-layouts  12.5 us
  transfers between devices with their start and end apart: 4, of which 4 were waited for; matrix products, arithmetic and copies ran while one was open for 7% of the time, Pallas kernels for 0%

commit v1 on v0

--- a/solution.py
+++ b/solution.py
@@ -32,7 +32,7 @@
         projected,
         lax.all_gather(scaled, "dp", axis=2, tiled=True).astype(jnp.float32),
     )
-    totals = lax.psum(partial_value, "tensor")
+    totals = jnp.sum(lax.all_gather(partial_value, "tensor"), axis=0)
     norm_factor = (act_proj.shape[1] * out_basis_t.shape[1] * seq_len) ** (-0.5)
     return totals * norm_factor
 

time: 475 us -> 450 us (0.947)
  the two profiles are of different devices: /device:TPU:64 before, /device:TPU:16 now
where the time goes in v1:
time: 450 us
  waiting for transfers between devices  338 us (75%)
  blocking collectives  49.1 us (11%)
  matrix products  34.6 us (8%)
  between operations  13.8 us (3%)
  local copies, waits for them, and re-layouts  12.8 us (3%)
    all_gather x1, waiting for transfers between devices, local(): full_act = lax.all_gather(activations, 'tensor', axis=1, tiled=True)  104 us
    all_gather x1, waiting for transfers between devices, local(): lax.all_gather(out_grads_t, 'tensor', axis=0, tiled=True)  101 us
    all_gather x1, waiting for transfers between devices, local(): act_proj = lax.all_gather(act_local, 'tensor', axis=1, tiled=True)  80.4 us
    all_gather x1, waiting for transfers between devices, local(): lax.all_gather(scaled, 'dp', axis=2, tiled=True).astype(jnp.float32)  51.5 us
    all_gather x1, blocking collectives, local(): totals = jnp.sum(lax.all_gather(partial_value, 'tensor'), axis=0)  49.1 us
    dot_general x1, matrix products, local(): jnp.einsum('sij,qij->sq', projected, lax.all_gather(scaled, 'dp', axis=2,...  15.5 us
    unnamed x9, local copies, waits for them, and re-layouts  12.5 us
  transfers between devices with their start and end apart: 4, of which 4 were waited for; matrix products, arithmetic and copies ran while one was open for 7% of the time, Pallas kernels for 0%

profile of v1, /device:TPU:16, one launch (start us, length us, event | category | flops | bytes accessed | tf_op | source)
XLA Modules:
  0.0 449.7 jit_solution(1590170188183974755)
XLA Ops:
  6.5 0.0 copy-start
  6.5 0.0 copy-start.2
  6.5 0.0 copy-start.1
  6.5 0.0 copy-start.3
  6.5 0.0 all-gather.8.cloned.1.call-start
  6.6 0.7 all-gather.8.cloned.1.call-update
  7.3 0.0 all-gather.14.cloned.1.call-start
  7.3 0.7 all-gather.14.cloned.1.call-update
  8.0 0.0 all-gather.10.cloned.1.call-start
  8.1 103.5 %all-gather.8.cloned.1.call-done = bf16[768,4096]{1,0:T(8,128)(2,1)} async-done(((bf16[768,128]{1,0:T(8,128)(2,1)}), bf16[768,4096]{1,0:T(8,128)(2,1)}) %all-gather.8.cloned.1.call-update) | async-done | bytes 6291472 | tf_op jit(solution)/shard_map/all_gather | solution.py:8
  111.6 5.5 %convolution_convert_fusion = bf16[768,128]{1,0:T(8,128)(2,1)} fusion(bf16[768,4096]{1,0:T(8,128)(2,1)} %all-gather.8.cloned.1.call-done, bf16[4096,128]{1,0:T(8,128)(2,1)} %param.10), kind=kOutput, calls=%fused_computation.4 | convolution fusion | flops 805404672 | bytes 7536640 | tf_op jit(solution)/shard_map/dot_general | solution.py:9
  117.1 0.0 all-gather.10.cloned.1.call-update
  117.1 0.0 all-gather.12.cloned.1.call-start
  117.8 0.0 copy-done.2
  117.9 0.0 copy-done.1
  117.9 0.9 fusion.6
  118.8 0.0 all-gather.12.cloned.1.call-update
  118.8 0.0 copy-done.3
  118.9 0.1 convert_bitcast_fusion
  118.9 100.7 %all-gather.14.cloned.1.call-done = bf16[32,172,768]{2,1,0:T(8,128)(2,1)} async-done(((bf16[1,172,768]{2,1,0:T(8,128)(2,1)}), bf16[32,172,768]{2,1,0:T(8,128)(2,1)}) %all-gather.14.cloned.1.call-update) | async-done | bytes 8454160 | tf_op jit(solution)/shard_map/all_gather | solution.py:15
  219.7 12.5 %reshape.31 = bf16[5504,768]{1,0:T(8,128)(2,1)} reshape(bf16[32,172,768]{2,1,0:T(8,128)(2,1)} %all-gather.14.cloned.1.call-done) | data formatting | bytes 16908288
  232.1 0.0 copy-done
  232.1 5.1 %fusion.2 = bf16[172,768]{1,0:T(8,128)(2,1)S(1)} fusion(bf16[172,5504]{1,0:T(8,128)(2,1)S(1)} %copy-done, bf16[5504,768]{1,0:T(8,128)(2,1)} %reshape.31, f32[768]{0:T(1024)S(1)} %convert_bitcast_fusion), kind=kOutput, calls=%fused_computation.3 | convolution fusion | flops 1454376960 | bytes 10614784 | tf_op jit(solution)/shard_map/dot_general | solution.py:13
  237.3 0.3 reshape.26
  237.6 80.4 %all-gather.10.cloned.1.call-done = bf16[768,4096]{1,0:T(8,128)(2,1)} async-done(((bf16[768,128]{1,0:T(8,128)(2,1)}), bf16[768,4096]{1,0:T(8,128)(2,1)}) %all-gather.10.cloned.1.call-update) | async-done | bytes 6291472 | tf_op jit(solution)/shard_map/all_gather | solution.py:10
  317.9 8.5 %fusion.7 = bf16[6,172,4096]{2,1,0:T(8,128)(2,1)} fusion(bf16[6,128,4096]{2,1,0:T(8,128)(2,1)} %bitcast.15, bf16[172,6,128]{2,1,0:T(8,128)(2,1)S(1)} %reshape.26), kind=kOutput, calls=%fused_computation.8 | convolution fusion | flops 1082130432 | bytes 15009792 | tf_op jit(solution)/shard_map/jst,std->sjd/dot_general | solution.py:24
  326.5 51.5 %all-gather.12.cloned.1.call-done = bf16[4,172,4096]{2,0,1:T(4,128)(2,1)} async-done(((bf16[4,172,256]{2,0,1:T(4,128)(2,1)}), bf16[4,172,4096]{2,0,1:T(4,128)(2,1)}) %all-gather.12.cloned.1.call-update) | async-done | bytes 5636112 | tf_op jit(solution)/shard_map/all_gather | solution.py:33
  378.0 15.5 %fusion.3 = f32[1,6,4]{1,2,0:T(4,128)S(1)} fusion(bf16[4,172,4096]{2,0,1:T(4,128)(2,1)} %all-gather.12.cloned.1.call-done, bf16[6,172,4096]{2,1,0:T(8,128)(2,1)} %fusion.7), kind=kOutput, calls=%fused_computation.5 | convolution fusion | flops 33816576 | bytes 14090336 | tf_op jit(solution)/shard_map/sij,qij->sq/dot_general | solution.py:30
  393.4 49.1 %all-gather.2 = f32[32,6,4]{1,2,0:T(4,128)S(1)} all-gather(f32[1,6,4]{1,2,0:T(4,128)S(1)} %fusion.3), channel_id=2, replica_groups=mesh['dp'=16,'tensor'=32] {'tensor'}, dimensions={0}, use_global_device_ids=true | all-gather | bytes 3168 | tf_op jit(solution)/shard_map/all_gather | solution.py:35
  442.6 0.6 broadcast_multiply_fusion
  (2 shorter events, 0.1 us)
Async XLA Ops:
  6.5 225.6 %copy-start = (bf16[172,5504]{1,0:T(8,128)(2,1)S(1)}, bf16[172,5504]{1,0:T(8,128)(2,1)}, u32[]{:S(2)}) copy-start(bf16[172,5504]{1,0:T(8,128)(2,1)} %param.11) | copy-start | bytes 5680132
  6.5 111.3 %copy-start.2 = (f32[172,256]{1,0:T(8,128)S(1)}, f32[172,256]{1,0:T(8,128)}, u32[]{:S(2)}) copy-start(f32[172,256]{1,0:T(8,128)} %param.13) | copy-start | bytes 528388
  6.5 111.3 %copy-start.1 = (bf16[4,172,256]{2,0,1:T(4,128)(2,1)S(1)}, bf16[4,172,256]{2,0,1:T(4,128)(2,1)}, u32[]{:S(2)}) copy-start(bf16[4,172,256]{2,0,1:T(4,128)(2,1)} %param.12) | copy-start | bytes 1056772
  6.5 112.3 %copy-start.3 = (s32[6]{0:T(128)S(1)}, s32[6]{0:T(128)}, u32[]{:S(2)}) copy-start(s32[6]{0:T(128)} %param.15) | copy-start | bytes 76
  6.5 105.1 %all-gather.8.cloned.1.call-start = ((), (), s32[]{:S(2)}) async-start(), calls=%async_computation | async-start | bytes 6488064 | tf_op jit(solution)/shard_map/all_gather | solution.py:8
  7.3 212.4 %all-gather.14.cloned.1.call-start = ((), (), s32[]{:S(2)}) async-start(), calls=%async_computation.3 | async-start | bytes 8921088 | tf_op jit(solution)/shard_map/all_gather | solution.py:15
  8.0 309.9 %all-gather.10.cloned.1.call-start = ((), (), s32[]{:S(2)}) async-start(), calls=%async_computation.1 | async-start | bytes 6488064 | tf_op jit(solution)/shard_map/all_gather | solution.py:10
  117.1 260.8 %all-gather.12.cloned.1.call-start = ((), (), s32[]{:S(2)}) async-start(), calls=%async_computation.2 | async-start | bytes 5988352 | tf_op jit(solution)/shard_map/all_gather | solution.py:33
Sparse Core Ops, SparseCore 0:
  10.4 101.1 all-gather.7
  114.8 104.8 all-gather.13
  222.7 95.1 all-gather.9
  319.8 58.0 all-gather.11
